TPU v7x, 32 devices: a whole 2x2x4 slice. The times are simulated.
32 devices in a mesh: dom: 8 (over y, x, core), cls: 4 (over z).
Axes of the slice: x: 2, y: 2, z: 4, core: 2. Of those that a mesh axis runs over, the one named last changes fastest.
Arguments:
- images: bfloat16 [1024, 64, 256], P('dom'), may hold values from -48 to 48
- class_refs: bfloat16 [64, 64, 256], P('cls', 'dom'), may hold values from -1 to 1
- ctf_table: float32 [64, 64], replicated, may hold values from 0.1 to 1
- ctf_group: int32 [1024], P('dom'), may hold values from 0 to 63
- prior_angle: int32 [1024], P('dom'), may hold values from 0 to 255
- precision: float32 [1024], P('dom'), may hold values from 0.25 to 4
Outputs:
- new_refs: float32 [64, 64, 256], P('cls', 'dom')
- log_evidence: float32 [1024], P('dom')
All inputs are finite; a program needn't handle non-finite values.
Results may differ from a plain program's by a relative error of at most 0.007.
Values may be sent and summed in bfloat16 or wider, within the bound.
A program may use at most 128 MiB of HBM per device.

v0:
```python
import math

import jax
import jax.numpy as jnp
from jax import lax
from jax.sharding import PartitionSpec as P

prior_strength = 2.0
ridge = 1.0
highest = lax.Precision.HIGHEST


def angle_table(angle_count, mode_count):
    angles = jnp.arange(angle_count, dtype=jnp.int32)
    freqs = jnp.arange(mode_count, dtype=jnp.int32)
    product = angles[:, None] * freqs[None, :] % angle_count
    phase = product.astype(jnp.float32) * (2.0 * math.pi / angle_count)
    return jnp.concatenate([jnp.cos(phase), jnp.sin(phase)], axis=1)


def split_table(forward):
    upper = forward.astype(jnp.bfloat16)
    lower = (forward - upper.astype(jnp.float32)).astype(jnp.bfloat16)
    return (upper, lower)


def mode_weights(angle_count, mode_count):
    freqs = jnp.arange(mode_count, dtype=jnp.int32)
    single = jnp.where(freqs == 0, 1.0, 2.0).astype(jnp.float32) / angle_count
    return jnp.concatenate([single, single])


def synthesis_table(angle_count, mode_count):
    return (
        jnp.transpose(angle_table(angle_count, mode_count))
        * mode_weights(angle_count, mode_count)[:, None]
    )


def spectrum(values, forward_pair):
    upper, lower = forward_pair
    flat = values.reshape(-1, values.shape[-1])
    result = jnp.dot(flat, upper, preferred_element_type=jnp.float32)
    result = result + jnp.dot(flat, lower, preferred_element_type=jnp.float32)
    return result.reshape(values.shape[:-1] + (upper.shape[1],))


def weighted_spectrum(images, ctf_rows, forward_pair):
    return (ctf_rows[:, :, None] * spectrum(images, forward_pair)).astype(jnp.bfloat16)


def prior_term(prior_angle, angle_count):
    rotations = jnp.arange(angle_count, dtype=jnp.int32)
    offsets = (rotations[None, :] - prior_angle[:, None]) % angle_count
    return prior_strength * jnp.cos(offsets.astype(jnp.float32) * (2.0 * math.pi / angle_count))


def pair_refs(spec_four):
    cos_part = spec_four[:, :, 0]
    sin_part = spec_four[:, :, 1]
    first_pair = jnp.stack([cos_part, sin_part], axis=2)
    second_pair = jnp.stack([-sin_part, cos_part], axis=2)
    return jnp.stack([first_pair, second_pair], axis=1)


def pair_weights(spec_four):
    cos_part = spec_four[:, :, 0]
    sin_part = spec_four[:, :, 1]
    first_pair = jnp.stack([cos_part, sin_part], axis=2)
    second_pair = jnp.stack([-sin_part, cos_part], axis=2)
    return jnp.stack([first_pair, second_pair], axis=2)


def local(images, class_refs, ctf_table, ctf_group, prior_angle, precision):
    particle_count, cycle_count, angle_count = images.shape
    mode_count = angle_count // 2
    class_count = class_refs.shape[0]
    forward = angle_table(angle_count, mode_count)
    forward_pair = split_table(forward)
    synthesis = synthesis_table(angle_count, mode_count)
    ref_local = spectrum(class_refs, forward_pair).astype(jnp.bfloat16)
    ref_spectra = lax.all_gather(ref_local, "dom", axis=1, tiled=True)
    group_ids = jnp.arange(ctf_table.shape[0], dtype=jnp.int32)
    one_hot = (ctf_group[:, None] == group_ids[None, :]).astype(jnp.float32)
    ctf_rows = jnp.dot(one_hot, ctf_table, precision=highest, preferred_element_type=jnp.float32)
    ctf_square = ctf_rows * ctf_rows
    particle_spectra = weighted_spectrum(images, ctf_rows, forward_pair)
    ref_float = ref_spectra.astype(jnp.float32)
    cycle_energy = jnp.sum(ref_float * ref_float * mode_weights(angle_count, mode_count), axis=2)
    energy = jnp.dot(
        ctf_square,
        jnp.transpose(cycle_energy),
        precision=highest,
        preferred_element_type=jnp.float32,
    )
    particle_four = particle_spectra.reshape(particle_count, cycle_count, 2, mode_count)
    ref_pairs = pair_refs(ref_spectra.reshape(class_count, cycle_count, 2, mode_count))
    cross = jnp.einsum(
        "prhm,kjrhm->pkjm", particle_four, ref_pairs, preferred_element_type=jnp.float32
    )
    correlation = jnp.dot(
        cross.reshape(-1, angle_count),
        synthesis,
        precision=highest,
        preferred_element_type=jnp.float32,
    )
    correlation = correlation.reshape(particle_count, class_count, angle_count)
    score = precision[:, None, None] * (correlation - 0.5 * energy[:, :, None])
    score = score + prior_term(prior_angle, angle_count)[:, None, :]
    row_top = jnp.max(score, axis=(1, 2))
    peak = lax.pmax(row_top, "cls")
    local_sum = jnp.sum(jnp.exp(score - peak[:, None, None]), axis=(1, 2))
    sum_exp = lax.psum(local_sum, "cls")
    log_evidence = peak + jnp.log(sum_exp)
    weights = jnp.exp(score - log_evidence[:, None, None]).astype(jnp.bfloat16)
    weight_spectra = spectrum(weights, forward_pair).astype(jnp.bfloat16)
    mass = jnp.sum(weights.astype(jnp.float32), axis=2)
    weight_pairs = pair_weights(weight_spectra.reshape(particle_count, class_count, 2, mode_count))
    class_sums = jnp.einsum(
        "pkjhm,prhm->rkjm", weight_pairs, particle_four, preferred_element_type=jnp.float32
    )
    class_sums = class_sums.reshape(cycle_count, class_count, angle_count)
    totals = jnp.dot(
        jnp.transpose(ctf_square), mass, precision=highest, preferred_element_type=jnp.float32
    )
    whole_sums, whole_totals = lax.psum((class_sums, totals), "dom")
    cycle_share = cycle_count // lax.axis_size("dom")
    cycle_start = lax.axis_index("dom") * cycle_share
    cycle_sums = lax.dynamic_slice_in_dim(whole_sums, cycle_start, cycle_share, 0)
    cycle_totals = lax.dynamic_slice_in_dim(whole_totals, cycle_start, cycle_share, 0)
    new_spectra = cycle_sums / (cycle_totals + ridge)[:, :, None]
    new_refs = jnp.dot(
        new_spectra.reshape(-1, angle_count),
        synthesis,
        precision=highest,
        preferred_element_type=jnp.float32,
    )
    new_refs = jnp.transpose(
        new_refs.reshape(cycle_sums.shape[0], class_count, angle_count), (1, 0, 2)
    )
    return (new_refs, log_evidence)


def solution(mesh):
    in_specs = (P("dom", None, None), P("cls", "dom", None), P(), P("dom"), P("dom"), P("dom"))
    out_specs = (P("cls", "dom", None), P("dom"))
    return jax.shard_map(local, mesh=mesh, in_specs=in_specs, out_specs=out_specs, check_vma=False)
```

profile of v0, /device:TPU:1, one launch (start us, length us, event | category | flops | bytes accessed | tf_op | source)
XLA Modules:
  0.0 186.8 jit_solution(16948213473205160676)
XLA Ops:
  7.2 0.5 fusion.46
  8.3 12.3 %all_gather.3 = bf16[16,64,256]{2,1,0:T(8,128)(2,1)S(1)} all-gather(bf16[16,8,256]{2,1,0:T(8,128)(2,1)S(1)} %fusion.18), channel_id=1, replica_groups=mesh['dom'=8,'cls'=4] {'dom'}, dimensions={1}, use_global_device_ids=true | all-gather | bytes 589824 | tf_op jit(solution)/shard_map/all_gather | solution.py:82
  20.9 3.6 %fusion.62 = f32[256,8192]{1,0:T(8,128)S(1)} fusion(bf16[8192,256]{1,0:T(8,128)(2,1)} %bitcast.52, f32[256,128]{1,0:T(8,128)S(1)} %get-tuple-element.18, f32[256,128]{1,0:T(8,128)S(1)} %get-tuple-element.19), kind=kOutput, calls=%fused_computation.82 | convolution fusion | flops 1074003968 | bytes 12845056 | tf_op jit(solution)/shard_map/dot_general | solution.py:43
  24.6 4.5 %fusion = f32[8192,256]{0,1:T(8,128)} fusion(f32[256,8192]{1,0:T(8,128)S(1)} %fusion.62, bf16[8192,256]{1,0:T(8,128)(2,1)S(1)} %bitcast.53, f32[256,128]{1,0:T(8,128)S(1)} %get-tuple-element.18, f32[256,128]{1,0:T(8,128)S(1)} %get-tuple-element.19), kind=kOutput, calls=%fused_computation.1 | convolution fusion | flops 1076166656 | bytes 21233664 | tf_op jit(solution)/shard_map/dot_general | solution.py:44
  29.1 14.2 %reshape.100 = f32[128,64,2,128]{1,0,3,2:T(8,128)} reshape(f32[8192,256]{0,1:T(8,128)} %fusion) | data formatting | bytes 16777216 | tf_op jit(solution)/shard_map/reshape | solution.py:45
  43.3 14.1 %copy.45 = f32[128,64,2,128]{3,1,2,0:T(8,128)} copy(f32[128,64,2,128]{1,0,3,2:T(8,128)} %reshape.100) | data formatting | bytes 16777216 | tf_op jit(solution)/shard_map/reshape | solution.py:45
  57.7 5.6 %fusion.1 = bf16[128,64,2,128,1]{3,1,2,0,4:T(8,128)(2,1)} fusion(f32[128,64,2,128]{3,1,2,0:T(8,128)} %copy.45, f32[128,64]{1,0:T(8,128)S(1)} %copy.43), kind=kLoop, calls=%fused_computation.3 | loop fusion | flops 4194304 | bytes 12615680 | tf_op jit(solution)/shard_map/convert_element_type | solution.py:49
  63.3 7.4 %copy.62 = bf16[128,64,2,128,1]{0,1,2,4,3:T(8,128)(2,1)} copy(bf16[128,64,2,128,1]{3,1,2,0,4:T(8,128)(2,1)} %fusion.1) | data formatting | bytes 8388608 | tf_op jit(solution)/shard_map/convert_element_type | solution.py:49
  70.7 1.2 fusion.30
  72.3 1.1 fusion.65
  73.5 0.5 copy.71
  74.0 0.5 copy.70
  74.7 1.3 copy.48
  76.2 3.5 %fusion.14 = f32[128,16,2,128]{0,1,2,3:T(8,128)S(1)} fusion(bf16[128,64,2,128,1]{0,1,2,4,3:T(8,128)(2,1)} %copy.62, bf16[16,1,64,2,128]{2,0,3,1,4:T(8,128)(2,1)S(1)} %maximum_bitcast_fusion, bf16[16,1,64,2,128]{2,0,3,1,4:T(8,128)(2,1)S(1)} %copy.48), kind=kOutput, calls=%fused_computation.19 | convolution fusion | flops 134742016 | bytes 7340032 | tf_op jit(solution)/shard_map/prhm,kjrhm->pkjm/dot_general | solution.py:98
  79.7 1.2 copy.50
  80.9 4.2 %fusion.66 = (f32[128]{0:T(128)S(1)}, f32[128,16,256]{2,0,1:T(8,128)S(1)}) fusion(f32[128,256]{1,0:T(8,128)S(1)} %copy-done.4, f32[128,16]{0,1:T(8,128)S(1)} %convolution_multiply_fusion, f32[128,16,256]{0,2,1:T(8,128)S(1)} %bitcast.56, f32[256]{0:T(256)S(1)} %pad_maximum_fusion.3, f32[256,128]{1,0:T(8,128)S(1)} %get-tuple-element.18, ...), kind=kOutput, calls=%fused_computation.85 | convolution fusion | flops 1612840832 | bytes 4597760 | tf_op jit(solution)/shard_map/dot_general | solution.py:101
  85.1 9.9 %pmax.7 = f32[128]{0:T(128)S(1)} all-reduce(f32[128]{0:T(128)S(1)} %get-tuple-element.16), channel_id=1, replica_groups=mesh['dom'=8,'cls'=4] {'cls'}, use_global_device_ids=true, to_apply=%region_2.3 | all-reduce | flops 128 | bytes 1024 | tf_op jit(solution)/shard_map/pmax | solution.py:111
  95.5 6.9 %psum.21 = f32[128]{0:T(128)S(1)} all-reduce(f32[128]{0:T(128)S(1)} %exponential_reduce_fusion), channel_id=1, replica_groups=mesh['dom'=8,'cls'=4] {'cls'}, use_global_device_ids=true, to_apply=%region_4.5 | all-reduce | flops 128 | bytes 1024 | tf_op jit(solution)/shard_map/psum | solution.py:113
  102.3 0.5 convert_reduce_fusion
  102.8 0.6 copy.52
  104.9 2.3 %fusion.64 = (bf16[128,16,1,128]{3,2,1,0:T(2,128)(2,1)S(1)}, bf16[128,16,1,128]{3,2,1,0:T(2,128)(2,1)}) fusion(bf16[128,16,2,128]{3,2,1,0:T(2,128)(2,1)S(1)} %convert_element_type.73), kind=kLoop, calls=%fused_computation.83 | loop fusion | bytes 2097152 | tf_op jit(solution)/shard_map/slice | solution.py:68
  107.2 1.8 copy.73
  108.9 0.8 copy.72
  109.9 2.3 %copy.55 = bf16[128,16,1,2,128]{0,1,3,2,4:T(8,128)(2,1)} copy(bf16[128,16,1,2,128]{4,3,1,0,2:T(2,128)(2,1)S(1)} %convert_element_type.72) | data formatting | bytes 2097152 | tf_op jit(solution)/shard_map/convert_element_type | solution.py:116
  112.3 1.1 copy-done.3
  113.4 3.4 %fusion.11 = f32[64,16,2,128]{0,1,2,3:T(8,128)S(1)} fusion(bf16[128,64,2,128,1]{0,1,2,4,3:T(8,128)(2,1)} %copy.62, bf16[128,16,1,2,128]{0,1,3,2,4:T(8,128)(2,1)S(1)} %maximum_bitcast_fusion.1, bf16[128,16,1,2,128]{0,1,3,2,4:T(8,128)(2,1)S(1)} %copy-done.3), kind=kOutput, calls=%fused_computation.18 | convolution fusion | flops 138412032 | bytes 7340032 | tf_op jit(solution)/shard_map/pkjhm,prhm->rkjm/dot_general | solution.py:119
  116.8 1.6 copy.57
  118.4 1.9 %reshape.94 = f32[64,16,256]{2,1,0:T(8,128)} reshape(f32[64,16,2,128]{3,2,1,0:T(2,128)S(1)} %copy.57) | data formatting | bytes 2097152 | tf_op jit(solution)/shard_map/reshape | solution.py:122
  120.5 23.3 %psum.23 = f32[64,16]{1,0:T(8,128)S(1)} all-reduce(f32[64,16]{1,0:T(8,128)S(1)} %fusion.50), channel_id=1, replica_groups=mesh['dom'=8,'cls'=4] {'dom'}, use_global_device_ids=true, to_apply=%region_7.8 | all-reduce | flops 1024 | bytes 8192 | tf_op jit(solution)/shard_map/psum | solution.py:126
  143.8 34.1 %all-reduce.2.cloned.1.call-done = f32[64,16,256]{2,1,0:T(8,128)} async-done(((f32[64,16,256]{2,1,0:T(8,128)}), f32[64,16,256]{2,1,0:T(8,128)}) %all-reduce.2.cloned.1.call-update) | async-done | bytes 1048592 | tf_op jit(solution)/shard_map/psum | solution.py:126
  177.9 1.3 convolution_bitcast_fusion
  179.2 0.7 copy.58
  (43 shorter events, 4.2 us)
Async XLA Ops:
  7.2 0.8 copy-start
  7.2 170.7 %all-reduce.2.cloned.1.call-start = ((), (), s32[]{:S(2)}) async-start(), calls=%async_computation | async-start | bytes 2097152 | tf_op jit(solution)/shard_map/psum | solution.py:126
  20.9 3.7 %copy-start.2 = (bf16[128,64,256]{2,1,0:T(8,128)(2,1)S(1)}, bf16[128,64,256]{2,1,0:T(8,128)(2,1)}, u32[]{:S(2)}) copy-start(bf16[128,64,256]{2,1,0:T(8,128)(2,1)} %param.6) | copy-start | bytes 12582916
  43.3 14.1 %copy-start.5 = (f32[64,64]{1,0:T(8,128)S(1)}, f32[64,64]{1,0:T(8,128)}, u32[]{:S(2)}) copy-start(f32[64,64]{1,0:T(8,128)} %param.8) | copy-start | bytes 49156
  43.3 14.1 %copy-start.6 = (s32[128]{0:T(128)S(1)}, s32[128]{0:T(128)}, u32[]{:S(2)}) copy-start(s32[128]{0:T(128)} %param.9) | copy-start | bytes 1540
  63.3 7.4 %copy-start.7 = (s32[128]{0:T(128)S(1)}, s32[128]{0:T(128)}, u32[]{:S(2)}) copy-start(s32[128]{0:T(128)} %param.10) | copy-start | bytes 1540
  79.6 1.2 copy-start.4
  79.6 1.2 copy-start.8
  102.3 1.1 copy-start.9
  112.2 1.2 copy-start.3
  116.8 63.1 %copy-start.1 = (bf16[16,8,256]{2,1,0:T(8,128)(2,1)S(1)}, bf16[16,8,256]{2,1,0:T(8,128)(2,1)}, u32[]{:S(2)}) copy-start(bf16[16,8,256]{2,1,0:T(8,128)(2,1)} %param.7) | copy-start | bytes 196612
Sparse Core Ops, SparseCore 0:
  120.5 57.3 all-reduce.1
where the time goes:
time: 189 us; the launch traced here: 187 us
  local copies, waits for them, and re-layouts  54.7 us (29%)
  blocking collectives  52.3 us (28%)
  waiting for transfers between devices  34.1 us (18%)
  matrix products  22.3 us (12%)
  between operations  14.3 us (8%)
  other arithmetic  8.97 us (5%)
    psum x1, waiting for transfers between devices, local(): whole_sums, whole_totals = lax.psum((class_sums, totals), 'dom')  34.1 us
    reshape x2, local copies, waits for them, and re-layouts, spectrum(): return result.reshape(values.shape[:-1] + (upper.shape[1],))  28.3 us
    psum x1, blocking collectives, local(): whole_sums, whole_totals = lax.psum((class_sums, totals), 'dom')  23.3 us
    all_gather x1, blocking collectives, local(): ref_spectra = lax.all_gather(ref_local, 'dom', axis=1, tiled=True)  12.3 us
    pmax x1, blocking collectives, local(): peak = lax.pmax(row_top, 'cls')  9.94 us
    convert_element_type x1, local copies, waits for them, and re-layouts, weighted_spectrum(): (ctf_rows[:, :, None] * spectrum(images, forward_pair)).astype(jnp.bfloat16)  7.41 us
    psum x1, blocking collectives, local(): sum_exp = lax.psum(local_sum, 'cls')  6.85 us
    unnamed x25, local copies, waits for them, and re-layouts  5.84 us
  transfers between devices with their start and end apart: 1, of which 1 were waited for; matrix products, arithmetic and copies ran while one was open for 0% of the time, Pallas kernels for 0%

commit v1 on v0

--- a/solution.py
+++ b/solution.py
@@ -1,8 +1,13 @@
+import functools
 import math
 
 import jax
 import jax.numpy as jnp
+import ml_dtypes
+import numpy as np
 from jax import lax
+from jax.experimental import pallas as pl
+from jax.experimental.pallas import tpu as pltpu
 from jax.sharding import PartitionSpec as P
 
 prior_strength = 2.0
@@ -141,7 +146,298 @@
     return (new_refs, log_evidence)
 
 
+def nt(left, right, precision=None):
+    return lax.dot_general(
+        left,
+        right,
+        (((1,), (1,)), ((), ())),
+        precision=precision,
+        preferred_element_type=jnp.float32,
+    )
+
+
+def nn(left, right, precision=None):
+    return jnp.dot(left, right, precision=precision, preferred_element_type=jnp.float32)
+
+
+def halves(value):
+    upper = value.astype(jnp.bfloat16)
+    lower = (value - upper.astype(jnp.float32)).astype(jnp.bfloat16)
+    return upper, lower
+
+
+def rounded(value):
+    return value.astype(jnp.bfloat16).astype(jnp.float32)
+
+
+def host_tables(angle_count, mode_count):
+    product = np.outer(np.arange(angle_count), np.arange(mode_count)) % angle_count
+    phase = product * (2.0 * math.pi / angle_count)
+    forward = np.concatenate([np.cos(phase), np.sin(phase)], axis=1).astype(np.float32)
+    single = np.where(np.arange(mode_count) == 0, 1.0, 2.0) / angle_count
+    scale = np.concatenate([single, single]).astype(np.float32)
+    inverse = forward * scale[None, :]
+
+    def split(table):
+        upper = table.astype(ml_dtypes.bfloat16)
+        lower = (table - upper.astype(np.float32)).astype(ml_dtypes.bfloat16)
+        return upper, lower
+
+    return split(np.ascontiguousarray(forward.T)) + split(inverse)
+
+
+def whole_kernel(
+    dom_size, cls_size, img, refs, table, group, angle, prec, fwd_hi, fwd_lo, inv_hi, inv_lo,
+    out_new, out_log, ref_slots, ref_rows, ctf, spec, ref_spec, cross, score, sums, send, recv,
+    tot_send, tot_recv, stat_send, stat_recv, ref_sems, stat_sems, sum_sems, tot_sems,
+):
+    mesh_ids = pl.DeviceIdType.MESH
+    dom, cls = lax.axis_index("dom"), lax.axis_index("cls")
+    parts, cycles, angles = img.shape
+    modes = angles // 2
+    share = cycles // dom_size
+    classes = refs.shape[0] // share
+    barrier = pltpu.get_barrier_semaphore()
+    for step in range(1, dom_size):
+        pl.semaphore_signal(barrier, inc=1, device_id={"dom": lax.rem(dom + step, dom_size)}, device_id_type=mesh_ids)
+    for step in range(1, cls_size):
+        pl.semaphore_signal(barrier, inc=1, device_id={"cls": lax.rem(cls + step, cls_size)}, device_id_type=mesh_ids)
+    pl.semaphore_wait(barrier, dom_size + cls_size - 2)
+
+    def remote(source, target, sems, axis, place, size, step):
+        return pltpu.make_async_remote_copy(
+            src_ref=source,
+            dst_ref=target,
+            send_sem=sems.at[0, step],
+            recv_sem=sems.at[1, step],
+            device_id={axis: lax.rem(place + step, size)},
+            device_id_type=mesh_ids,
+        )
+
+    ref_copies = [
+        remote(refs, ref_slots.at[step], ref_sems, "dom", dom, dom_size, step)
+        for step in range(1, dom_size)
+    ]
+    for copy in ref_copies:
+        copy.start()
+
+    lanes = lax.broadcasted_iota(jnp.int32, (modes, modes), 1)
+    low = lanes < cycles
+    groups = lax.broadcasted_iota(jnp.int32, (parts, table.shape[0]), 1)
+    one_hot = (groups == group[...]).astype(jnp.float32)
+    ctf[...] = nn(one_hot, table[...], highest)
+
+    def transform(block):
+        result = nt(fwd_hi[...], block) + nt(fwd_lo[...], block)
+        found = []
+        for pair in range(2):
+            top = result[:modes, pair * modes : (pair + 1) * modes]
+            bottom = result[modes:, pair * modes : (pair + 1) * modes]
+            found.append(jnp.where(low, top, pltpu.roll(bottom, cycles, 1)))
+            found.append(jnp.where(low, pltpu.roll(top, cycles, 1), bottom))
+        return found
+
+    def image_step(step, carry):
+        first = step * 4
+        block = img[pl.ds(first, 4)].reshape(4 * cycles, angles)
+        for offset, value in enumerate(transform(block)):
+            row = ctf[pl.ds(first + offset, 1), :]
+            spec[pl.ds(first + offset, modes, stride=parts), :] = value * row
+        return carry
+
+    lax.fori_loop(0, parts // 4, image_step, 0, unroll=2)
+
+    for copy in ref_copies:
+        copy.wait()
+    for step in range(dom_size):
+        source = refs[...] if step == 0 else ref_slots[step]
+        source = source.astype(jnp.float32).reshape(classes, share, angles)
+        owner = lax.rem(dom - step + dom_size, dom_size)
+        ref_rows[:, pl.ds(pl.multiple_of(owner * share, share), share), :] = source
+    rows = lax.broadcasted_iota(jnp.int32, (modes, modes), 0)
+    weight = jnp.where(rows == 0, 1.0, 2.0) * (1.0 / angles)
+    sign = jnp.where(lax.broadcasted_iota(jnp.int32, (classes, modes), 1) < cycles, 1.0, -1.0)
+    energies = []
+    for step in range(classes // 4):
+        block = ref_rows[step * 4 : step * 4 + 4].reshape(4 * cycles, angles).astype(jnp.bfloat16)
+        for offset, value in enumerate(transform(block)):
+            index = step * 4 + offset
+            value = rounded(value)
+            energies.append(jnp.sum(value * value * weight, axis=0, keepdims=True))
+            ref_spec[pl.ds(index, modes, stride=2 * classes), :] = value
+            turned = pltpu.roll(value, cycles, 1)
+            ref_spec[pl.ds(classes + index, modes, stride=2 * classes), :] = jnp.where(low, -turned, turned)
+    ctf_square = ctf[...] * ctf[...]
+    energy = nt(jnp.concatenate(energies, axis=0), ctf_square, highest)
+
+    def cross_step(mode, carry):
+        particles = spec[pl.ds(pl.multiple_of(mode * parts, parts), parts), :].astype(jnp.bfloat16)
+        others = ref_spec[pl.ds(pl.multiple_of(mode * 2 * classes, 2 * classes), 2 * classes), :]
+        cross[pl.ds(mode, 2 * classes, stride=modes), :] = nt(others.astype(jnp.bfloat16), particles)
+        return carry
+
+    lax.fori_loop(0, modes, cross_step, 0, unroll=8)
+
+    turns = lax.broadcasted_iota(jnp.int32, (angles, parts), 0)
+    offsets = (turns - angle[...] + angles) % angles
+    prior = prior_strength * jnp.cos(offsets.astype(jnp.float32) * (2.0 * math.pi / angles))
+    scale = prec[...]
+    peak = None
+    for index in range(classes):
+        both = jnp.concatenate(
+            [cross[index * modes : (index + 1) * modes, :],
+             cross[(classes + index) * modes : (classes + index + 1) * modes, :]], axis=0)
+        upper, lower = halves(both)
+        found = nn(inv_hi[...], upper) + (nn(inv_hi[...], lower) + nn(inv_lo[...], upper))
+        found = scale * (found - 0.5 * energy[index : index + 1, :]) + prior
+        score[index] = found
+        top = jnp.max(found, axis=0, keepdims=True)
+        peak = top if peak is None else jnp.maximum(peak, top)
+    total = jnp.zeros((1, parts), jnp.float32)
+    for index in range(classes):
+        total = total + jnp.sum(jnp.exp(score[index] - peak), axis=0, keepdims=True)
+    stat_send[...] = jnp.concatenate([peak] * 4 + [total] * 4, axis=0)
+    stat_copies = [
+        remote(stat_send, stat_recv.at[step], stat_sems, "cls", cls, cls_size, step)
+        for step in range(1, cls_size)
+    ]
+    for copy in stat_copies:
+        copy.start()
+    for copy in stat_copies:
+        copy.wait()
+    pairs = [(peak, total)]
+    for step in range(1, cls_size):
+        pairs.append((stat_recv[step, 0:1, :], stat_recv[step, 4:5, :]))
+    best = peak
+    for other, _ in pairs[1:]:
+        best = jnp.maximum(best, other)
+    whole = jnp.zeros((1, parts), jnp.float32)
+    for other, part in pairs:
+        whole = whole + part * jnp.exp(other - best)
+    log_evidence = best + jnp.log(whole)
+    out_log[...] = log_evidence
+
+    masses = []
+    for index in range(classes):
+        weights = jnp.exp(score[index] - log_evidence).astype(jnp.bfloat16)
+        masses.append(jnp.sum(weights.astype(jnp.float32), axis=0, keepdims=True))
+        found = nn(fwd_hi[...], weights) + nn(fwd_lo[...], weights)
+        cross[index * modes : (index + 1) * modes, :] = found[:modes]
+        cross[(classes + index) * modes : (classes + index + 1) * modes, :] = found[modes:]
+    tot_send[...] = nn(jnp.concatenate(masses, axis=0), ctf_square, highest)
+    tot_copies = [
+        remote(tot_send, tot_recv.at[step], tot_sems, "dom", dom, dom_size, step)
+        for step in range(1, dom_size)
+    ]
+    for copy in tot_copies:
+        copy.start()
+
+    def sum_step(mode, carry):
+        particles = spec[pl.ds(pl.multiple_of(mode * parts, parts), parts), :].astype(jnp.bfloat16)
+        weights = cross[pl.ds(mode, 2 * classes, stride=modes), :].astype(jnp.bfloat16)
+        found = nn(weights, particles)
+        found = found[:classes] + sign * pltpu.roll(found[classes:], cycles, 1)
+        sums[pl.ds(mode, classes, stride=modes), :] = found
+        return carry
+
+    lax.fori_loop(0, modes, sum_step, 0, unroll=8)
+
+    for index in range(classes):
+        turned = jnp.transpose(sums[index * modes : (index + 1) * modes, :])
+        for part in range(dom_size):
+            piece = jnp.concatenate(
+                [turned[part * share : (part + 1) * share],
+                 turned[cycles + part * share : cycles + (part + 1) * share]], axis=0)
+            send[part, index * 2 * share : (index + 1) * 2 * share, :] = piece.astype(jnp.bfloat16)
+    sum_copies = [
+        remote(send.at[lax.rem(dom + step, dom_size)], recv.at[step], sum_sems, "dom", dom, dom_size, step)
+        for step in range(1, dom_size)
+    ]
+    for copy in sum_copies:
+        copy.start()
+    for copy in tot_copies:
+        copy.wait()
+    totals = tot_send[...]
+    for step in range(1, dom_size):
+        totals = totals + tot_recv[step]
+    columns = lax.broadcasted_iota(jnp.int32, (1, share, modes), 2)
+    wanted = lax.broadcasted_iota(jnp.int32, (1, share, modes), 1) + dom * share
+    picked = jnp.where(columns == wanted, totals[:, None, :], 0.0)
+    divisor = jnp.sum(picked, axis=2, keepdims=True).reshape(classes * share, 1) + ridge
+    for copy in sum_copies:
+        copy.wait()
+    gathered = send[dom].astype(jnp.float32)
+    for step in range(1, dom_size):
+        gathered = gathered + recv[step].astype(jnp.float32)
+    gathered = gathered.reshape(classes, 2, share, modes)
+    result = jnp.zeros((classes * share, angles), jnp.float32)
+    for half in range(2):
+        upper, lower = halves(gathered[:, half].reshape(classes * share, modes))
+        hi = inv_hi[:, half * modes : (half + 1) * modes]
+        lo = inv_lo[:, half * modes : (half + 1) * modes]
+        result = result + nt(upper, hi) + (nt(lower, hi) + nt(upper, lo))
+    out_new[...] = result / divisor
+
+
+def fused(images, class_refs, ctf_table, ctf_group, prior_angle, precision):
+    dom_size, cls_size = lax.axis_size("dom"), lax.axis_size("cls")
+    parts, cycles, angles = images.shape
+    modes = angles // 2
+    classes, share, _ = class_refs.shape
+    tables = host_tables(angles, modes)
+    f32, bf16 = jnp.float32, jnp.bfloat16
+    vmem = pl.BlockSpec(memory_space=pltpu.VMEM)
+    new_refs, log_evidence = pl.pallas_call(
+        functools.partial(whole_kernel, dom_size, cls_size),
+        out_shape=(
+            jax.ShapeDtypeStruct((classes * share, angles), f32),
+            jax.ShapeDtypeStruct((1, parts), f32),
+        ),
+        in_specs=[vmem] * 10,
+        out_specs=(vmem, vmem),
+        scratch_shapes=[
+            pltpu.VMEM((dom_size, classes * share, angles), bf16),
+            pltpu.VMEM((classes, cycles, angles), f32),
+            pltpu.VMEM((parts, modes), f32),
+            pltpu.VMEM((modes * parts, modes), f32),
+            pltpu.VMEM((modes * 2 * classes, modes), f32),
+            pltpu.VMEM((2 * classes * modes, parts), f32),
+            pltpu.VMEM((classes, angles, parts), f32),
+            pltpu.VMEM((classes * modes, modes), f32),
+            pltpu.VMEM((dom_size, classes * 2 * share, modes), bf16),
+            pltpu.VMEM((dom_size, classes * 2 * share, modes), bf16),
+            pltpu.VMEM((classes, modes), f32),
+            pltpu.VMEM((dom_size, classes, modes), f32),
+            pltpu.VMEM((8, parts), f32),
+            pltpu.VMEM((cls_size, 8, parts), f32),
+            pltpu.SemaphoreType.DMA((2, dom_size)),
+            pltpu.SemaphoreType.DMA((2, cls_size)),
+            pltpu.SemaphoreType.DMA((2, dom_size)),
+            pltpu.SemaphoreType.DMA((2, dom_size)),
+        ],
+        compiler_params=pltpu.CompilerParams(
+            collective_id=0, has_side_effects=True, vmem_limit_bytes=52 * 1024 * 1024
+        ),
+    )(
+        images,
+        class_refs.reshape(classes * share, angles),
+        jnp.concatenate([ctf_table, ctf_table], axis=1),
+        ctf_group[:, None],
+        prior_angle[None, :],
+        precision[None, :],
+        *[jnp.asarray(table) for table in tables],
+    )
+    return new_refs.reshape(classes, share, angles), log_evidence.reshape(parts)
+
+
+def pick(images, class_refs, *rest):
+    parts, cycles, angles = images.shape
+    classes, share, _ = class_refs.shape
+    fits = angles == 256 and cycles == 64 and parts == 128 and share % 8 == 0 and classes % 16 == 0
+    return (fused if fits else local)(images, class_refs, *rest)
+
+
 def solution(mesh):
     in_specs = (P("dom", None, None), P("cls", "dom", None), P(), P("dom"), P("dom"), P("dom"))
     out_specs = (P("cls", "dom", None), P("dom"))
-    return jax.shard_map(local, mesh=mesh, in_specs=in_specs, out_specs=out_specs, check_vma=False)
+    return jax.shard_map(pick, mesh=mesh, in_specs=in_specs, out_specs=out_specs, check_vma=False)

time: 189 us -> 55.6 us (0.29)
  blocking collectives: 52.3 us -> 0 us
  local copies, waits for them, and re-layouts: 54.7 us -> 7.69 us
  Pallas kernels: 0 us -> 45.9 us
  waiting for transfers between devices: 34.1 us -> 0 us
  matrix products: 22.3 us -> 0 us
  between operations: 14.3 us -> 0.65 us
  other arithmetic: 8.97 us -> 0.91 us
    pallas_call x0 -> x1, Pallas kernels: none -> 45.9 us  [fused(): pl.pallas_call(functools.partial(whole_kernel, dom_size, cls_size), out_s...]
    psum x1 -> x0, waiting for transfers between devices: 34.1 us -> none  [local(): whole_sums, whole_totals = lax.psum((class_sums, totals), 'dom')]
    reshape x4 -> x0, local copies, waits for them, and re-layouts: 30.3 us -> none  [the longest x2 28.3 us: spectrum(): return result.reshape(values.shape[:-1] + (upper.shape[1],))]
    psum x2 -> x0, blocking collectives: 30.1 us -> none  [the longest x1 23.3 us: local(): whole_sums, whole_totals = lax.psum((class_sums, totals), 'dom')]
    dot_general x13 -> x0, matrix products: 22.3 us -> none  [the longest x3 5.14 us: spectrum(): result = result + jnp.dot(flat, lower, preferred_element_type=jnp.float32)]
    all_gather x1 -> x0, blocking collectives: 12.3 us -> none  [local(): ref_spectra = lax.all_gather(ref_local, 'dom', axis=1, tiled=True)]
    convert_element_type x5 -> x0, local copies, waits for them, and re-layouts: 10.9 us -> none  [the longest x1 7.41 us: weighted_spectrum(): (ctf_rows[:, :, None] * spectrum(images, forward_pair)).astype(jnp.bfloat16)]
    pmax x1 -> x0, blocking collectives: 9.94 us -> none  [local(): peak = lax.pmax(row_top, 'cls')]
  transfers between devices with their start and end apart: 1 -> 0, of which waited for: 1 -> 0; matrix products, arithmetic and copies ran while one was open for 0% -> 0% of each run, Pallas kernels for 0% -> 0%
where the time goes in v1:
time: 55.6 us; the launch traced here: 55.2 us
  Pallas kernels  45.9 us (83%)
  local copies, waits for them, and re-layouts  7.69 us (14%)
  other arithmetic  0.91 us (2%)
  between operations  0.65 us (1%)
    pallas_call x1, Pallas kernels, fused(): pl.pallas_call(functools.partial(whole_kernel, dom_size, cls_size), out_s...  45.9 us
    unnamed x16, local copies, waits for them, and re-layouts  6.93 us

profile of v1, /device:TPU:1, one launch (start us, length us, event | category | flops | bytes accessed | tf_op | source)
XLA Modules:
  0.0 55.2 jit_solution(7426952625494198339)
XLA Ops:
  0.6 0.9 %pad_maximum_fusion.table = f32[64,128]{1,0:T(8,128)S(1)} fusion(f32[64,64]{1,0:T(8,128)} %param.12), kind=kLoop, calls=%fused_computation | loop fusion | flops 8192 | bytes 49152 | tf_op jit(solution)/shard_map/concatenate | solution.py:424
  1.5 0.8 %copy.12.group = s32[128,1]{1,0:T(8,128)S(1)} copy(s32[128,1]{0,1:T(1,128)} %bitcast.11) | data formatting | bytes 1024 | tf_op jit(solution)/shard_map/broadcast_in_dim | solution.py:425
  2.3 0.0 copy-start
  2.3 0.9 %copy-done = bf16[256,256]{1,0:T(8,128)(2,1)S(1)} copy-done((bf16[256,256]{1,0:T(8,128)(2,1)S(1)}, bf16[256,256]{1,0:T(8,128)(2,1)}, u32[]{:S(2)}) %copy-start) | copy-done | bytes 131096
  3.2 0.0 copy-start.1
  3.2 0.9 %copy-done.1 = bf16[256,256]{1,0:T(8,128)(2,1)S(1)} copy-done((bf16[256,256]{1,0:T(8,128)(2,1)S(1)}, bf16[256,256]{1,0:T(8,128)(2,1)}, u32[]{:S(2)}) %copy-start.1) | copy-done | bytes 131096
  4.1 0.0 copy-start.2
  4.1 0.9 %copy-done.2 = bf16[256,256]{1,0:T(8,128)(2,1)S(1)} copy-done((bf16[256,256]{1,0:T(8,128)(2,1)S(1)}, bf16[256,256]{1,0:T(8,128)(2,1)}, u32[]{:S(2)}) %copy-start.2) | copy-done | bytes 131096
  5.0 0.0 copy-start.3
  5.0 0.9 %copy-done.3 = bf16[256,256]{1,0:T(8,128)(2,1)S(1)} copy-done((bf16[256,256]{1,0:T(8,128)(2,1)S(1)}, bf16[256,256]{1,0:T(8,128)(2,1)}, u32[]{:S(2)}) %copy-start.3) | copy-done | bytes 131096
  5.9 0.0 copy-start.4
  5.9 0.8 %copy-done.4 = bf16[16,8,256]{2,1,0:T(8,128)(2,1)S(1)} copy-done((bf16[16,8,256]{2,1,0:T(8,128)(2,1)S(1)}, bf16[16,8,256]{2,1,0:T(8,128)(2,1)}, u32[]{:S(2)}) %copy-start.4) | copy-done | bytes 65560
  6.8 0.0 copy-start.5
  6.8 0.7 %copy-done.5 = s32[128]{0:T(128)S(1)} copy-done((s32[128]{0:T(128)S(1)}, s32[128]{0:T(128)}, u32[]{:S(2)}) %copy-start.5) | copy-done | bytes 536
  7.4 0.0 copy-start.6
  7.4 0.7 %copy-done.6 = f32[128]{0:T(128)S(1)} copy-done((f32[128]{0:T(128)S(1)}, f32[128]{0:T(128)}, u32[]{:S(2)}) %copy-start.6) | copy-done | bytes 536
  8.1 45.9 %shard_map.113 = (f32[128,256]{1,0:T(8,128)S(1)}, f32[1,128]{1,0:T(1,128)S(1)}) custom-call(bf16[128,64,256]{2,1,0:T(8,128)(2,1)} %img.1, bf16[128,256]{1,0:T(8,128)(2,1)S(1)} %bitcast.7, f32[64,128]{1,0:T(8,128)S(1)} %pad_maximum_fusion.table, s32[128,1]{1,0:T(8,128)S(1)} %copy.12.group, s32[1,128]{1,0:T(1,128)S(1)} %bitcast.8, f32[1,128]{1,0:T(1,128)S(1)} %bitcast.9, ...), custom_call_target="tpu_custom_call" | custom-call | tf_op jit(solution)/shard_map/pallas_call | solution.py:390
  54.0 0.7 %copy.15 = f32[16,8,256]{2,1,0:T(8,128)} copy(f32[16,8,256]{2,1,0:T(8,128)S(1)} %bitcast.6) | data formatting | bytes 262144
  54.7 0.5 copy.16
Async XLA Ops:
  2.3 0.9 %copy-start = (bf16[256,256]{1,0:T(8,128)(2,1)S(1)}, bf16[256,256]{1,0:T(8,128)(2,1)}, u32[]{:S(2)}) copy-start(bf16[256,256]{1,0:T(8,128)(2,1)} %constant.11.clone.inv_lo) | copy-start | bytes 393220
  3.2 0.9 %copy-start.1 = (bf16[256,256]{1,0:T(8,128)(2,1)S(1)}, bf16[256,256]{1,0:T(8,128)(2,1)}, u32[]{:S(2)}) copy-start(bf16[256,256]{1,0:T(8,128)(2,1)} %constant.10.clone.inv_hi) | copy-start | bytes 393220
  4.1 0.9 %copy-start.2 = (bf16[256,256]{1,0:T(8,128)(2,1)S(1)}, bf16[256,256]{1,0:T(8,128)(2,1)}, u32[]{:S(2)}) copy-start(bf16[256,256]{1,0:T(8,128)(2,1)} %constant.9.clone.fwd_lo) | copy-start | bytes 393220
  5.0 0.9 %copy-start.3 = (bf16[256,256]{1,0:T(8,128)(2,1)S(1)}, bf16[256,256]{1,0:T(8,128)(2,1)}, u32[]{:S(2)}) copy-start(bf16[256,256]{1,0:T(8,128)(2,1)} %constant.8.clone.fwd_hi) | copy-start | bytes 393220
  5.9 0.8 %copy-start.4 = (bf16[16,8,256]{2,1,0:T(8,128)(2,1)S(1)}, bf16[16,8,256]{2,1,0:T(8,128)(2,1)}, u32[]{:S(2)}) copy-start(bf16[16,8,256]{2,1,0:T(8,128)(2,1)} %param.11) | copy-start | bytes 196612
  6.8 0.7 %copy-start.5 = (s32[128]{0:T(128)S(1)}, s32[128]{0:T(128)}, u32[]{:S(2)}) copy-start(s32[128]{0:T(128)} %param.14) | copy-start | bytes 1540
  7.4 0.7 %copy-start.6 = (f32[128]{0:T(128)S(1)}, f32[128]{0:T(128)}, u32[]{:S(2)}) copy-start(f32[128]{0:T(128)} %param.15) | copy-start | bytes 1540

commit v2 on v1

--- a/solution.py
+++ b/solution.py
@@ -146,6 +146,13 @@
     return (new_refs, log_evidence)
 
 
+gap = 8
+
+
+def block_at(index, size):
+    return slice(index * (size + gap), index * (size + gap) + size)
+
+
 def nt(left, right, precision=None):
     return lax.dot_general(
         left,
@@ -202,7 +209,6 @@
         pl.semaphore_signal(barrier, inc=1, device_id={"dom": lax.rem(dom + step, dom_size)}, device_id_type=mesh_ids)
     for step in range(1, cls_size):
         pl.semaphore_signal(barrier, inc=1, device_id={"cls": lax.rem(cls + step, cls_size)}, device_id_type=mesh_ids)
-    pl.semaphore_wait(barrier, dom_size + cls_size - 2)
 
     def remote(source, target, sems, axis, place, size, step):
         return pltpu.make_async_remote_copy(
@@ -218,9 +224,6 @@
         remote(refs, ref_slots.at[step], ref_sems, "dom", dom, dom_size, step)
         for step in range(1, dom_size)
     ]
-    for copy in ref_copies:
-        copy.start()
-
     lanes = lax.broadcasted_iota(jnp.int32, (modes, modes), 1)
     low = lanes < cycles
     groups = lax.broadcasted_iota(jnp.int32, (parts, table.shape[0]), 1)
@@ -242,10 +245,19 @@
         block = img[pl.ds(first, 4)].reshape(4 * cycles, angles)
         for offset, value in enumerate(transform(block)):
             row = ctf[pl.ds(first + offset, 1), :]
-            spec[pl.ds(first + offset, modes, stride=parts), :] = value * row
+            spec[pl.ds(first + offset, modes, stride=parts + gap), :] = value * row
         return carry
 
-    lax.fori_loop(0, parts // 4, image_step, 0, unroll=2)
+    early = parts // 16
+    lax.fori_loop(0, early, image_step, 0, unroll=4)
+    pl.semaphore_wait(barrier, dom_size + cls_size - 2)
+    for copy in ref_copies:
+        copy.start()
+    lax.fori_loop(early, parts // 4, image_step, 0, unroll=4)
+
+    turns = lax.broadcasted_iota(jnp.int32, (angles, parts), 0)
+    offsets = (turns - angle[...] + angles) % angles
+    prior = prior_strength * jnp.cos(offsets.astype(jnp.float32) * (2.0 * math.pi / angles))
 
     for copy in ref_copies:
         copy.wait()
@@ -264,29 +276,26 @@
             index = step * 4 + offset
             value = rounded(value)
             energies.append(jnp.sum(value * value * weight, axis=0, keepdims=True))
-            ref_spec[pl.ds(index, modes, stride=2 * classes), :] = value
+            ref_spec[pl.ds(index, modes, stride=2 * classes + gap), :] = value
             turned = pltpu.roll(value, cycles, 1)
-            ref_spec[pl.ds(classes + index, modes, stride=2 * classes), :] = jnp.where(low, -turned, turned)
+            ref_spec[pl.ds(classes + index, modes, stride=2 * classes + gap), :] = jnp.where(low, -turned, turned)
     ctf_square = ctf[...] * ctf[...]
     energy = nt(jnp.concatenate(energies, axis=0), ctf_square, highest)
 
     def cross_step(mode, carry):
-        particles = spec[pl.ds(pl.multiple_of(mode * parts, parts), parts), :].astype(jnp.bfloat16)
-        others = ref_spec[pl.ds(pl.multiple_of(mode * 2 * classes, 2 * classes), 2 * classes), :]
-        cross[pl.ds(mode, 2 * classes, stride=modes), :] = nt(others.astype(jnp.bfloat16), particles)
+        particles = spec[pl.ds(pl.multiple_of(mode * (parts + gap), gap), parts), :].astype(jnp.bfloat16)
+        others = ref_spec[pl.ds(pl.multiple_of(mode * (2 * classes + gap), gap), 2 * classes), :]
+        cross[pl.ds(mode, 2 * classes, stride=modes + gap), :] = nt(others.astype(jnp.bfloat16), particles)
         return carry
 
-    lax.fori_loop(0, modes, cross_step, 0, unroll=8)
-
-    turns = lax.broadcasted_iota(jnp.int32, (angles, parts), 0)
-    offsets = (turns - angle[...] + angles) % angles
-    prior = prior_strength * jnp.cos(offsets.astype(jnp.float32) * (2.0 * math.pi / angles))
+    lax.fori_loop(0, modes, cross_step, 0, unroll=32)
+
     scale = prec[...]
     peak = None
     for index in range(classes):
         both = jnp.concatenate(
-            [cross[index * modes : (index + 1) * modes, :],
-             cross[(classes + index) * modes : (classes + index + 1) * modes, :]], axis=0)
+            [cross[block_at(index, modes), :],
+             cross[block_at(classes + index, modes), :]], axis=0)
         upper, lower = halves(both)
         found = nn(inv_hi[...], upper) + (nn(inv_hi[...], lower) + nn(inv_lo[...], upper))
         found = scale * (found - 0.5 * energy[index : index + 1, :]) + prior
@@ -322,8 +331,8 @@
         weights = jnp.exp(score[index] - log_evidence).astype(jnp.bfloat16)
         masses.append(jnp.sum(weights.astype(jnp.float32), axis=0, keepdims=True))
         found = nn(fwd_hi[...], weights) + nn(fwd_lo[...], weights)
-        cross[index * modes : (index + 1) * modes, :] = found[:modes]
-        cross[(classes + index) * modes : (classes + index + 1) * modes, :] = found[modes:]
+        cross[block_at(index, modes), :] = found[:modes]
+        cross[block_at(classes + index, modes), :] = found[modes:]
     tot_send[...] = nn(jnp.concatenate(masses, axis=0), ctf_square, highest)
     tot_copies = [
         remote(tot_send, tot_recv.at[step], tot_sems, "dom", dom, dom_size, step)
@@ -333,17 +342,17 @@
         copy.start()
 
     def sum_step(mode, carry):
-        particles = spec[pl.ds(pl.multiple_of(mode * parts, parts), parts), :].astype(jnp.bfloat16)
-        weights = cross[pl.ds(mode, 2 * classes, stride=modes), :].astype(jnp.bfloat16)
+        particles = spec[pl.ds(pl.multiple_of(mode * (parts + gap), gap), parts), :].astype(jnp.bfloat16)
+        weights = cross[pl.ds(mode, 2 * classes, stride=modes + gap), :].astype(jnp.bfloat16)
         found = nn(weights, particles)
         found = found[:classes] + sign * pltpu.roll(found[classes:], cycles, 1)
-        sums[pl.ds(mode, classes, stride=modes), :] = found
+        sums[pl.ds(mode, classes, stride=modes + gap), :] = found
         return carry
 
-    lax.fori_loop(0, modes, sum_step, 0, unroll=8)
+    lax.fori_loop(0, modes, sum_step, 0, unroll=32)
 
     for index in range(classes):
-        turned = jnp.transpose(sums[index * modes : (index + 1) * modes, :])
+        turned = jnp.transpose(sums[block_at(index, modes), :])
         for part in range(dom_size):
             piece = jnp.concatenate(
                 [turned[part * share : (part + 1) * share],
@@ -399,11 +408,11 @@
             pltpu.VMEM((dom_size, classes * share, angles), bf16),
             pltpu.VMEM((classes, cycles, angles), f32),
             pltpu.VMEM((parts, modes), f32),
-            pltpu.VMEM((modes * parts, modes), f32),
-            pltpu.VMEM((modes * 2 * classes, modes), f32),
-            pltpu.VMEM((2 * classes * modes, parts), f32),
+            pltpu.VMEM((modes * (parts + gap), modes), f32),
+            pltpu.VMEM((modes * (2 * classes + gap), modes), f32),
+            pltpu.VMEM((2 * classes * (modes + gap), parts), f32),
             pltpu.VMEM((classes, angles, parts), f32),
-            pltpu.VMEM((classes * modes, modes), f32),
+            pltpu.VMEM((classes * (modes + gap), modes), f32),
             pltpu.VMEM((dom_size, classes * 2 * share, modes), bf16),
             pltpu.VMEM((dom_size, classes * 2 * share, modes), bf16),
             pltpu.VMEM((classes, modes), f32),

time: 55.6 us -> 45 us (0.81)
  Pallas kernels: 45.9 us -> 35.4 us
    pallas_call x1, Pallas kernels: 45.9 us -> 35.4 us  [fused(): pl.pallas_call(functools.partial(whole_kernel, dom_size, cls_size), out_s...]
where the time goes in v2:
time: 45 us; the launch traced here: 44.7 us
  Pallas kernels  35.4 us (79%)
  local copies, waits for them, and re-layouts  7.69 us (17%)
  other arithmetic  0.91 us (2%)
  between operations  0.65 us (1%)
    pallas_call x1, Pallas kernels, fused(): pl.pallas_call(functools.partial(whole_kernel, dom_size, cls_size), out_s...  35.4 us
    unnamed x16, local copies, waits for them, and re-layouts  6.93 us
    concatenate x1, other arithmetic, fused(): jnp.concatenate([ctf_table, ctf_table], axis=1)  0.91 us

profile of v2, /device:TPU:1, one launch (start us, length us, event | category | flops | bytes accessed | tf_op | source)
XLA Modules:
  0.0 44.7 jit_solution(6184055393723053046)
XLA Ops:
  0.6 0.9 %pad_maximum_fusion.table = f32[64,128]{1,0:T(8,128)S(1)} fusion(f32[64,64]{1,0:T(8,128)} %param.12), kind=kLoop, calls=%fused_computation | loop fusion | flops 8192 | bytes 49152 | tf_op jit(solution)/shard_map/concatenate | solution.py:433
  1.5 0.8 %copy.12.group = s32[128,1]{1,0:T(8,128)S(1)} copy(s32[128,1]{0,1:T(1,128)} %bitcast.11) | data formatting | bytes 1024 | tf_op jit(solution)/shard_map/broadcast_in_dim | solution.py:434
  2.3 0.0 copy-start
  2.3 0.9 %copy-done = bf16[256,256]{1,0:T(8,128)(2,1)S(1)} copy-done((bf16[256,256]{1,0:T(8,128)(2,1)S(1)}, bf16[256,256]{1,0:T(8,128)(2,1)}, u32[]{:S(2)}) %copy-start) | copy-done | bytes 131096
  3.2 0.0 copy-start.1
  3.2 0.9 %copy-done.1 = bf16[256,256]{1,0:T(8,128)(2,1)S(1)} copy-done((bf16[256,256]{1,0:T(8,128)(2,1)S(1)}, bf16[256,256]{1,0:T(8,128)(2,1)}, u32[]{:S(2)}) %copy-start.1) | copy-done | bytes 131096
  4.1 0.0 copy-start.2
  4.1 0.9 %copy-done.2 = bf16[256,256]{1,0:T(8,128)(2,1)S(1)} copy-done((bf16[256,256]{1,0:T(8,128)(2,1)S(1)}, bf16[256,256]{1,0:T(8,128)(2,1)}, u32[]{:S(2)}) %copy-start.2) | copy-done | bytes 131096
  5.0 0.0 copy-start.3
  5.0 0.9 %copy-done.3 = bf16[256,256]{1,0:T(8,128)(2,1)S(1)} copy-done((bf16[256,256]{1,0:T(8,128)(2,1)S(1)}, bf16[256,256]{1,0:T(8,128)(2,1)}, u32[]{:S(2)}) %copy-start.3) | copy-done | bytes 131096
  5.9 0.0 copy-start.4
  5.9 0.8 %copy-done.4 = bf16[16,8,256]{2,1,0:T(8,128)(2,1)S(1)} copy-done((bf16[16,8,256]{2,1,0:T(8,128)(2,1)S(1)}, bf16[16,8,256]{2,1,0:T(8,128)(2,1)}, u32[]{:S(2)}) %copy-start.4) | copy-done | bytes 65560
  6.8 0.0 copy-start.5
  6.8 0.7 %copy-done.5 = s32[128]{0:T(128)S(1)} copy-done((s32[128]{0:T(128)S(1)}, s32[128]{0:T(128)}, u32[]{:S(2)}) %copy-start.5) | copy-done | bytes 536
  7.4 0.0 copy-start.6
  7.4 0.7 %copy-done.6 = f32[128]{0:T(128)S(1)} copy-done((f32[128]{0:T(128)S(1)}, f32[128]{0:T(128)}, u32[]{:S(2)}) %copy-start.6) | copy-done | bytes 536
  8.1 35.4 %shard_map.113 = (f32[128,256]{1,0:T(8,128)S(1)}, f32[1,128]{1,0:T(1,128)S(1)}) custom-call(bf16[128,64,256]{2,1,0:T(8,128)(2,1)} %img.1, bf16[128,256]{1,0:T(8,128)(2,1)S(1)} %bitcast.7, f32[64,128]{1,0:T(8,128)S(1)} %pad_maximum_fusion.table, s32[128,1]{1,0:T(8,128)S(1)} %copy.12.group, s32[1,128]{1,0:T(1,128)S(1)} %bitcast.8, f32[1,128]{1,0:T(1,128)S(1)} %bitcast.9, ...), custom_call_target="tpu_custom_call" | custom-call | tf_op jit(solution)/shard_map/pallas_call | solution.py:399
  43.5 0.7 %copy.15 = f32[16,8,256]{2,1,0:T(8,128)} copy(f32[16,8,256]{2,1,0:T(8,128)S(1)} %bitcast.6) | data formatting | bytes 262144
  44.1 0.5 %copy.16 = f32[128]{0:T(128)} copy(f32[128]{0:T(128)S(1)} %bitcast.10) | data formatting | bytes 1024
Async XLA Ops:
  2.3 0.9 %copy-start = (bf16[256,256]{1,0:T(8,128)(2,1)S(1)}, bf16[256,256]{1,0:T(8,128)(2,1)}, u32[]{:S(2)}) copy-start(bf16[256,256]{1,0:T(8,128)(2,1)} %constant.11.clone.inv_lo) | copy-start | bytes 393220
  3.2 0.9 %copy-start.1 = (bf16[256,256]{1,0:T(8,128)(2,1)S(1)}, bf16[256,256]{1,0:T(8,128)(2,1)}, u32[]{:S(2)}) copy-start(bf16[256,256]{1,0:T(8,128)(2,1)} %constant.10.clone.inv_hi) | copy-start | bytes 393220
  4.1 0.9 %copy-start.2 = (bf16[256,256]{1,0:T(8,128)(2,1)S(1)}, bf16[256,256]{1,0:T(8,128)(2,1)}, u32[]{:S(2)}) copy-start(bf16[256,256]{1,0:T(8,128)(2,1)} %constant.9.clone.fwd_lo) | copy-start | bytes 393220
  5.0 0.9 %copy-start.3 = (bf16[256,256]{1,0:T(8,128)(2,1)S(1)}, bf16[256,256]{1,0:T(8,128)(2,1)}, u32[]{:S(2)}) copy-start(bf16[256,256]{1,0:T(8,128)(2,1)} %constant.8.clone.fwd_hi) | copy-start | bytes 393220
  5.9 0.8 %copy-start.4 = (bf16[16,8,256]{2,1,0:T(8,128)(2,1)S(1)}, bf16[16,8,256]{2,1,0:T(8,128)(2,1)}, u32[]{:S(2)}) copy-start(bf16[16,8,256]{2,1,0:T(8,128)(2,1)} %param.11) | copy-start | bytes 196612
  6.8 0.7 %copy-start.5 = (s32[128]{0:T(128)S(1)}, s32[128]{0:T(128)}, u32[]{:S(2)}) copy-start(s32[128]{0:T(128)} %param.14) | copy-start | bytes 1540
  7.4 0.7 %copy-start.6 = (f32[128]{0:T(128)S(1)}, f32[128]{0:T(128)}, u32[]{:S(2)}) copy-start(f32[128]{0:T(128)} %param.15) | copy-start | bytes 1540

commit v3 on v2

--- a/solution.py
+++ b/solution.py
@@ -194,21 +194,37 @@
 
 
 def whole_kernel(
-    dom_size, cls_size, img, refs, table, group, angle, prec, fwd_hi, fwd_lo, inv_hi, inv_lo,
+    dom_size, cls_size, img_in, refs_in, table_in, group_in, angle_in, prec_in, fwd_hi_in, fwd_lo_in, inv_hi_in, inv_lo_in,
     out_new, out_log, ref_slots, ref_rows, ctf, spec, ref_spec, cross, score, sums, send, recv,
-    tot_send, tot_recv, stat_send, stat_recv, ref_sems, stat_sems, sum_sems, tot_sems,
+    tot_send, tot_recv, stat_send, stat_recv, img, table, group, angle, prec, fwd_hi, fwd_lo, inv_hi, inv_lo, load_sems, ref_sems, stat_sems, sum_sems, tot_sems,
 ):
     mesh_ids = pl.DeviceIdType.MESH
     dom, cls = lax.axis_index("dom"), lax.axis_index("cls")
-    parts, cycles, angles = img.shape
+    parts, cycles, angles = img_in.shape
     modes = angles // 2
     share = cycles // dom_size
-    classes = refs.shape[0] // share
+    classes = refs_in.shape[0] // share
     barrier = pltpu.get_barrier_semaphore()
     for step in range(1, dom_size):
         pl.semaphore_signal(barrier, inc=1, device_id={"dom": lax.rem(dom + step, dom_size)}, device_id_type=mesh_ids)
     for step in range(1, cls_size):
         pl.semaphore_signal(barrier, inc=1, device_id={"cls": lax.rem(cls + step, cls_size)}, device_id_type=mesh_ids)
+
+    early = parts // 16
+    pieces = [pl.ds(start, early * 4) for start in range(0, parts, early * 4)]
+    small = [
+        (table_in, table), (group_in, group), (fwd_hi_in, fwd_hi), (fwd_lo_in, fwd_lo),
+        (img_in.at[pieces[0]], img.at[pieces[0]]),
+    ]
+    late = [(img_in.at[piece], img.at[piece]) for piece in pieces[1:]] + [
+        (angle_in, angle), (prec_in, prec), (inv_hi_in, inv_hi), (inv_lo_in, inv_lo), (refs_in, ref_slots.at[0])
+    ]
+    loads = [
+        pltpu.make_async_copy(source, target, load_sems.at[place])
+        for place, (source, target) in enumerate(small + late)
+    ]
+    for load in loads:
+        load.start()
 
     def remote(source, target, sems, axis, place, size, step):
         return pltpu.make_async_remote_copy(
@@ -221,14 +237,19 @@
         )
 
     ref_copies = [
-        remote(refs, ref_slots.at[step], ref_sems, "dom", dom, dom_size, step)
+        remote(refs_in, ref_slots.at[step], ref_sems, "dom", dom, dom_size, step)
         for step in range(1, dom_size)
     ]
     lanes = lax.broadcasted_iota(jnp.int32, (modes, modes), 1)
     low = lanes < cycles
-    groups = lax.broadcasted_iota(jnp.int32, (parts, table.shape[0]), 1)
+    for load in loads[: len(small)]:
+        load.wait()
+    groups = lax.broadcasted_iota(jnp.int32, (table.shape[0], parts), 0)
     one_hot = (groups == group[...]).astype(jnp.float32)
-    ctf[...] = nn(one_hot, table[...], highest)
+    doubled = jnp.concatenate([table[...], table[...]], axis=1)
+    ctf[...] = lax.dot_general(
+        one_hot, doubled, (((0,), (0,)), ((), ())), precision=highest, preferred_element_type=jnp.float32
+    )
 
     def transform(block):
         result = nt(fwd_hi[...], block) + nt(fwd_lo[...], block)
@@ -248,11 +269,12 @@
             spec[pl.ds(first + offset, modes, stride=parts + gap), :] = value * row
         return carry
 
-    early = parts // 16
     lax.fori_loop(0, early, image_step, 0, unroll=4)
     pl.semaphore_wait(barrier, dom_size + cls_size - 2)
     for copy in ref_copies:
         copy.start()
+    for load in loads[len(small) :]:
+        load.wait()
     lax.fori_loop(early, parts // 4, image_step, 0, unroll=4)
 
     turns = lax.broadcasted_iota(jnp.int32, (angles, parts), 0)
@@ -262,8 +284,7 @@
     for copy in ref_copies:
         copy.wait()
     for step in range(dom_size):
-        source = refs[...] if step == 0 else ref_slots[step]
-        source = source.astype(jnp.float32).reshape(classes, share, angles)
+        source = ref_slots[step].astype(jnp.float32).reshape(classes, share, angles)
         owner = lax.rem(dom - step + dom_size, dom_size)
         ref_rows[:, pl.ds(pl.multiple_of(owner * share, share), share), :] = source
     rows = lax.broadcasted_iota(jnp.int32, (modes, modes), 0)
@@ -288,7 +309,7 @@
         cross[pl.ds(mode, 2 * classes, stride=modes + gap), :] = nt(others.astype(jnp.bfloat16), particles)
         return carry
 
-    lax.fori_loop(0, modes, cross_step, 0, unroll=32)
+    lax.fori_loop(0, modes, cross_step, 0, unroll=64)
 
     scale = prec[...]
     peak = None
@@ -349,7 +370,7 @@
         sums[pl.ds(mode, classes, stride=modes + gap), :] = found
         return carry
 
-    lax.fori_loop(0, modes, sum_step, 0, unroll=32)
+    lax.fori_loop(0, modes, sum_step, 0, unroll=64)
 
     for index in range(classes):
         turned = jnp.transpose(sums[block_at(index, modes), :])
@@ -402,7 +423,7 @@
             jax.ShapeDtypeStruct((classes * share, angles), f32),
             jax.ShapeDtypeStruct((1, parts), f32),
         ),
-        in_specs=[vmem] * 10,
+        in_specs=[pl.BlockSpec(memory_space=pltpu.HBM)] * 10,
         out_specs=(vmem, vmem),
         scratch_shapes=[
             pltpu.VMEM((dom_size, classes * share, angles), bf16),
@@ -419,6 +440,16 @@
             pltpu.VMEM((dom_size, classes, modes), f32),
             pltpu.VMEM((8, parts), f32),
             pltpu.VMEM((cls_size, 8, parts), f32),
+            pltpu.VMEM((parts, cycles, angles), bf16),
+            pltpu.VMEM(ctf_table.shape, f32),
+            pltpu.VMEM((1, parts), jnp.int32),
+            pltpu.VMEM((1, parts), jnp.int32),
+            pltpu.VMEM((1, parts), f32),
+            pltpu.VMEM((angles, angles), bf16),
+            pltpu.VMEM((angles, angles), bf16),
+            pltpu.VMEM((angles, angles), bf16),
+            pltpu.VMEM((angles, angles), bf16),
+            pltpu.SemaphoreType.DMA((16,)),
             pltpu.SemaphoreType.DMA((2, dom_size)),
             pltpu.SemaphoreType.DMA((2, cls_size)),
             pltpu.SemaphoreType.DMA((2, dom_size)),
@@ -430,8 +461,8 @@
     )(
         images,
         class_refs.reshape(classes * share, angles),
-        jnp.concatenate([ctf_table, ctf_table], axis=1),
-        ctf_group[:, None],
+        ctf_table,
+        ctf_group[None, :],
         prior_angle[None, :],
         precision[None, :],
         *[jnp.asarray(table) for table in tables],

time: 45 us -> 43 us (0.956)
  Pallas kernels: 35.4 us -> 33.6 us
  other arithmetic: 0.91 us -> 0 us
  local copies, waits for them, and re-layouts: 7.69 us -> 8.34 us
    pallas_call x1, Pallas kernels: 35.4 us -> 33.6 us  [fused(): pl.pallas_call(functools.partial(whole_kernel, dom_size, cls_size), out_s...]
    unnamed x16 -> x20, local copies, waits for them, and re-layouts: 6.93 us -> 8.34 us
    concatenate x1 -> x0, other arithmetic: 0.91 us -> none  [fused(): jnp.concatenate([ctf_table, ctf_table], axis=1)]
    broadcast_in_dim x1 -> x0, local copies, waits for them, and re-layouts: 0.76 us -> none  [fused(): ctf_group[:, None]]
where the time goes in v3:
time: 43 us; the launch traced here: 42.6 us
  Pallas kernels  33.6 us (78%)
  local copies, waits for them, and re-layouts  8.34 us (19%)
  between operations  0.66 us (2%)
    pallas_call x1, Pallas kernels, fused(): pl.pallas_call(functools.partial(whole_kernel, dom_size, cls_size), out_s...  33.6 us
    unnamed x20, local copies, waits for them, and re-layouts  8.34 us

profile of v3, /device:TPU:1, one launch (start us, length us, event | category | flops | bytes accessed | tf_op | source)
XLA Modules:
  0.0 42.6 jit_solution(16092645418787958151)
XLA Ops:
  0.6 0.0 copy-start
  0.6 0.9 %copy-done = bf16[256,256]{1,0:T(8,128)(2,1)S(1)} copy-done((bf16[256,256]{1,0:T(8,128)(2,1)S(1)}, bf16[256,256]{1,0:T(8,128)(2,1)}, u32[]{:S(2)}) %copy-start) | copy-done | bytes 131096
  1.5 0.0 copy-start.1
  1.5 0.9 %copy-done.1 = bf16[256,256]{1,0:T(8,128)(2,1)S(1)} copy-done((bf16[256,256]{1,0:T(8,128)(2,1)S(1)}, bf16[256,256]{1,0:T(8,128)(2,1)}, u32[]{:S(2)}) %copy-start.1) | copy-done | bytes 131096
  2.4 0.0 copy-start.2
  2.4 0.9 %copy-done.2 = bf16[256,256]{1,0:T(8,128)(2,1)S(1)} copy-done((bf16[256,256]{1,0:T(8,128)(2,1)S(1)}, bf16[256,256]{1,0:T(8,128)(2,1)}, u32[]{:S(2)}) %copy-start.2) | copy-done | bytes 131096
  3.3 0.0 copy-start.3
  3.4 0.9 %copy-done.3 = bf16[256,256]{1,0:T(8,128)(2,1)S(1)} copy-done((bf16[256,256]{1,0:T(8,128)(2,1)S(1)}, bf16[256,256]{1,0:T(8,128)(2,1)}, u32[]{:S(2)}) %copy-start.3) | copy-done | bytes 131096
  4.3 0.0 copy-start.4
  4.3 0.8 %copy-done.4 = bf16[16,8,256]{2,1,0:T(8,128)(2,1)S(1)} copy-done((bf16[16,8,256]{2,1,0:T(8,128)(2,1)S(1)}, bf16[16,8,256]{2,1,0:T(8,128)(2,1)}, u32[]{:S(2)}) %copy-start.4) | copy-done | bytes 65560
  5.1 0.0 copy-start.5
  5.1 0.8 %copy-done.5 = f32[64,64]{1,0:T(8,128)S(1)} copy-done((f32[64,64]{1,0:T(8,128)S(1)}, f32[64,64]{1,0:T(8,128)}, u32[]{:S(2)}) %copy-start.5) | copy-done | bytes 16408
  5.9 0.0 copy-start.6
  5.9 0.7 %copy-done.6 = s32[128]{0:T(128)S(1)} copy-done((s32[128]{0:T(128)S(1)}, s32[128]{0:T(128)}, u32[]{:S(2)}) %copy-start.6) | copy-done | bytes 536
  6.5 0.0 copy-start.7
  6.5 0.7 %copy-done.7 = s32[128]{0:T(128)S(1)} copy-done((s32[128]{0:T(128)S(1)}, s32[128]{0:T(128)}, u32[]{:S(2)}) %copy-start.7) | copy-done | bytes 536
  7.2 0.0 copy-start.8
  7.2 0.7 %copy-done.8 = f32[128]{0:T(128)S(1)} copy-done((f32[128]{0:T(128)S(1)}, f32[128]{0:T(128)}, u32[]{:S(2)}) %copy-start.8) | copy-done | bytes 536
  7.8 33.6 %shard_map.113 = (f32[128,256]{1,0:T(8,128)S(1)}, f32[1,128]{1,0:T(1,128)S(1)}) custom-call(bf16[128,64,256]{2,1,0:T(8,128)(2,1)} %img_in.1, bf16[128,256]{1,0:T(8,128)(2,1)S(1)} %bitcast.7, f32[64,64]{1,0:T(8,128)S(1)} %copy-done.5, s32[1,128]{1,0:T(1,128)S(1)} %bitcast.8, s32[1,128]{1,0:T(1,128)S(1)} %bitcast.9, f32[1,128]{1,0:T(1,128)S(1)} %bitcast.10, ...), custom_call_target="tpu_custom_call" | custom-call | tf_op jit(solution)/shard_map/pallas_call | solution.py:420
  41.5 0.7 %copy.14 = f32[16,8,256]{2,1,0:T(8,128)} copy(f32[16,8,256]{2,1,0:T(8,128)S(1)} %bitcast.6) | data formatting | bytes 262144
  42.1 0.5 %copy.15 = f32[128]{0:T(128)} copy(f32[128]{0:T(128)S(1)} %bitcast.11) | data formatting | bytes 1024
Async XLA Ops:
  0.6 0.9 %copy-start = (bf16[256,256]{1,0:T(8,128)(2,1)S(1)}, bf16[256,256]{1,0:T(8,128)(2,1)}, u32[]{:S(2)}) copy-start(bf16[256,256]{1,0:T(8,128)(2,1)} %constant.11.clone.inv_lo_in) | copy-start | bytes 393220
  1.5 0.9 %copy-start.1 = (bf16[256,256]{1,0:T(8,128)(2,1)S(1)}, bf16[256,256]{1,0:T(8,128)(2,1)}, u32[]{:S(2)}) copy-start(bf16[256,256]{1,0:T(8,128)(2,1)} %constant.10.clone.inv_hi_in) | copy-start | bytes 393220
  2.4 0.9 %copy-start.2 = (bf16[256,256]{1,0:T(8,128)(2,1)S(1)}, bf16[256,256]{1,0:T(8,128)(2,1)}, u32[]{:S(2)}) copy-start(bf16[256,256]{1,0:T(8,128)(2,1)} %constant.9.clone.fwd_lo_in) | copy-start | bytes 393220
  3.3 0.9 %copy-start.3 = (bf16[256,256]{1,0:T(8,128)(2,1)S(1)}, bf16[256,256]{1,0:T(8,128)(2,1)}, u32[]{:S(2)}) copy-start(bf16[256,256]{1,0:T(8,128)(2,1)} %constant.8.clone.fwd_hi_in) | copy-start | bytes 393220
  4.3 0.8 %copy-start.4 = (bf16[16,8,256]{2,1,0:T(8,128)(2,1)S(1)}, bf16[16,8,256]{2,1,0:T(8,128)(2,1)}, u32[]{:S(2)}) copy-start(bf16[16,8,256]{2,1,0:T(8,128)(2,1)} %param.11) | copy-start | bytes 196612
  5.1 0.8 %copy-start.5 = (f32[64,64]{1,0:T(8,128)S(1)}, f32[64,64]{1,0:T(8,128)}, u32[]{:S(2)}) copy-start(f32[64,64]{1,0:T(8,128)} %table_in.1) | copy-start | bytes 49156
  5.9 0.7 %copy-start.6 = (s32[128]{0:T(128)S(1)}, s32[128]{0:T(128)}, u32[]{:S(2)}) copy-start(s32[128]{0:T(128)} %param.13) | copy-start | bytes 1540
  6.5 0.7 %copy-start.7 = (s32[128]{0:T(128)S(1)}, s32[128]{0:T(128)}, u32[]{:S(2)}) copy-start(s32[128]{0:T(128)} %param.14) | copy-start | bytes 1540
  7.2 0.7 %copy-start.8 = (f32[128]{0:T(128)S(1)}, f32[128]{0:T(128)}, u32[]{:S(2)}) copy-start(f32[128]{0:T(128)} %param.15) | copy-start | bytes 1540

commit v4 on v3

--- a/solution.py
+++ b/solution.py
@@ -456,7 +456,7 @@
             pltpu.SemaphoreType.DMA((2, dom_size)),
         ],
         compiler_params=pltpu.CompilerParams(
-            collective_id=0, has_side_effects=True, vmem_limit_bytes=52 * 1024 * 1024
+            collective_id=0, has_side_effects=True, vmem_limit_bytes=63 * 1024 * 1024
         ),
     )(
         images,

time: 43 us -> 38.1 us (0.89)
  local copies, waits for them, and re-layouts: 8.34 us -> 2.74 us
  Pallas kernels: 33.6 us -> 34.5 us
    unnamed x20 -> x2, local copies, waits for them, and re-layouts: 8.34 us -> 2.74 us
    pallas_call x1, Pallas kernels: 33.6 us -> 34.5 us  [fused(): pl.pallas_call(functools.partial(whole_kernel, dom_size, cls_size), out_s...]
where the time goes in v4:
time: 38.1 us; the launch traced here: 37.9 us
  Pallas kernels  34.5 us (91%)
  local copies, waits for them, and re-layouts  2.74 us (7%)
  between operations  0.64 us (2%)
    pallas_call x1, Pallas kernels, fused(): pl.pallas_call(functools.partial(whole_kernel, dom_size, cls_size), out_s...  34.5 us
    unnamed x2, local copies, waits for them, and re-layouts  2.74 us

profile of v4, /device:TPU:1, one launch (start us, length us, event | category | flops | bytes accessed | tf_op | source)
XLA Modules:
  0.0 37.9 jit_solution(4654884894397982413)
XLA Ops:
  0.6 34.5 %shard_map.113 = (f32[128,256]{1,0:T(8,128)}, f32[1,128]{1,0:T(1,128)}) custom-call(bf16[128,64,256]{2,1,0:T(8,128)(2,1)} %img_in.1, bf16[128,256]{1,0:T(8,128)(2,1)} %bitcast.7, f32[64,64]{1,0:T(8,128)} %table_in.1, s32[1,128]{1,0:T(1,128)} %bitcast.8, s32[1,128]{1,0:T(1,128)} %bitcast.9, f32[1,128]{1,0:T(1,128)} %bitcast.10, ...), custom_call_target="tpu_custom_call" | custom-call | tf_op jit(solution)/shard_map/pallas_call | solution.py:420
  35.2 1.6 %copy.14 = f32[16,8,256]{2,1,0:T(8,128)} copy(f32[16,8,256]{2,1,0:T(8,128)} %bitcast.6) | data formatting | bytes 262144
  36.7 1.2 %copy.15 = f32[128]{0:T(128)} copy(f32[128]{0:T(128)} %bitcast.11) | data formatting | bytes 1024

commit v5 on v4

--- a/solution.py
+++ b/solution.py
@@ -269,13 +269,13 @@
             spec[pl.ds(first + offset, modes, stride=parts + gap), :] = value * row
         return carry
 
-    lax.fori_loop(0, early, image_step, 0, unroll=4)
+    lax.fori_loop(0, early, image_step, 0, unroll=8)
     pl.semaphore_wait(barrier, dom_size + cls_size - 2)
     for copy in ref_copies:
         copy.start()
     for load in loads[len(small) :]:
         load.wait()
-    lax.fori_loop(early, parts // 4, image_step, 0, unroll=4)
+    lax.fori_loop(early, parts // 4, image_step, 0, unroll=8)
 
     turns = lax.broadcasted_iota(jnp.int32, (angles, parts), 0)
     offsets = (turns - angle[...] + angles) % angles
@@ -309,7 +309,7 @@
         cross[pl.ds(mode, 2 * classes, stride=modes + gap), :] = nt(others.astype(jnp.bfloat16), particles)
         return carry
 
-    lax.fori_loop(0, modes, cross_step, 0, unroll=64)
+    lax.fori_loop(0, modes, cross_step, 0, unroll=128)
 
     scale = prec[...]
     peak = None
@@ -370,7 +370,7 @@
         sums[pl.ds(mode, classes, stride=modes + gap), :] = found
         return carry
 
-    lax.fori_loop(0, modes, sum_step, 0, unroll=64)
+    lax.fori_loop(0, modes, sum_step, 0, unroll=128)
 
     for index in range(classes):
         turned = jnp.transpose(sums[block_at(index, modes), :])

time: 38.1 us -> 37.2 us (0.976)
  Pallas kernels: 34.5 us -> 33.6 us
    pallas_call x1, Pallas kernels: 34.5 us -> 33.6 us  [fused(): pl.pallas_call(functools.partial(whole_kernel, dom_size, cls_size), out_s...]
where the time goes in v5:
time: 37.2 us; the launch traced here: 37 us
  Pallas kernels  33.6 us (90%)
  local copies, waits for them, and re-layouts  2.74 us (7%)
  between operations  0.64 us (2%)
    pallas_call x1, Pallas kernels, fused(): pl.pallas_call(functools.partial(whole_kernel, dom_size, cls_size), out_s...  33.6 us
    unnamed x2, local copies, waits for them, and re-layouts  2.74 us

profile of v5, /device:TPU:1, one launch (start us, length us, event | category | flops | bytes accessed | tf_op | source)
XLA Modules:
  0.0 37.0 jit_solution(10202784177339652690)
XLA Ops:
  0.6 33.6 %shard_map.113 = (f32[128,256]{1,0:T(8,128)}, f32[1,128]{1,0:T(1,128)}) custom-call(bf16[128,64,256]{2,1,0:T(8,128)(2,1)} %img_in.1, bf16[128,256]{1,0:T(8,128)(2,1)} %bitcast.7, f32[64,64]{1,0:T(8,128)} %table_in.1, s32[1,128]{1,0:T(1,128)} %bitcast.8, s32[1,128]{1,0:T(1,128)} %bitcast.9, f32[1,128]{1,0:T(1,128)} %bitcast.10, ...), custom_call_target="tpu_custom_call" | custom-call | tf_op jit(solution)/shard_map/pallas_call | solution.py:420
  34.3 1.6 %copy.14 = f32[16,8,256]{2,1,0:T(8,128)} copy(f32[16,8,256]{2,1,0:T(8,128)} %bitcast.6) | data formatting | bytes 262144
  35.8 1.2 %copy.15 = f32[128]{0:T(128)} copy(f32[128]{0:T(128)} %bitcast.11) | data formatting | bytes 1024
